TPU v7x, 256 devices: a whole 4x4x8 slice. The times are simulated.
256 devices in a mesh: vx: 16 (over z_lo, x, core), vy: 4 (over y), scan: 4 (over z_hi).
Axes of the slice: x: 4, y: 4, z: 8 (z_hi: 4, z_lo: 2; z = z_hi * 2 + z_lo), core: 2. Of those that a mesh axis runs over, the one named last changes fastest.
Arguments:
- volume: bfloat16 [2, 512, 256, 256], P(None, 'vx', 'vy'), may hold values from -6 to 6
- tile_matrix: bfloat16 [4, 16, 8, 1024, 128], P('scan', 'vx', 'vy'), may hold values from -0.03125 to 0.03125
- tile_offset: int32 [4, 16, 8], P('scan', 'vx', 'vy'), may hold values from 0 to 384
- patch_count: int32 [4, 64], P('scan', ('vx', 'vy')), may hold values from 1 to 3, as said below
- scan_position: int32 [4, 64, 3, 2], P('scan', ('vx', 'vy')), may hold values from 0 to 256, as said below
- measured: float32 [4, 64, 3, 256, 256], P('scan', ('vx', 'vy')), may hold values from 0.2 to 5
- illumination: float32 [2, 256, 256], replicated, may hold values from -6 to 6
Outputs:
- change: float32 [2, 512, 256, 256], P(None, 'vx', 'vy', 'scan')
Inputs may be any that keep to these rules, and one draw needn't show every extreme that they name: `patch_count`: an owner's slots below its count hold measured patches, the others are unused; at every angle some owner holds 3. `scan_position`: column 0 is a patch's first detector column, 0 to 256; column 1 its first row, 0 to 0.
All inputs are finite; a program needn't handle non-finite values.
Results may differ from a plain program's by a relative error of at most 0.0085.
Values may be sent and summed in bfloat16 or wider, within the bound.
A program may use at most 64 MiB of HBM per device.

v0:
```python
import functools
import math

import jax
import jax.numpy as jnp
import numpy as np
from jax import lax
from jax.experimental import pallas as pl
from jax.experimental.pallas import tpu as pltpu
from jax.sharding import PartitionSpec as P

MESH = pl.DeviceIdType.MESH
BF = jnp.bfloat16
F32 = jnp.float32

ABSORPTION = 0.2
STEP_LENGTH = 0.003
SIDE = 256
CAP = 3

PROJ_WIRE = BF
PROJ_FULL = F32
IMAGE_WIRE = BF

CORE_P, CORE_I = 0, 1
MATS = 2
OFFS = 8
RS_P, RS_I = 11, 23
Z_P = 35
Z_I = 36
AG_P, AG_I = 44, 56
CORE_GP, CORE_GI = 68, 69
N_SEMS = 70


def tables():
    n = np.arange(SIDE)
    angle = 2.0 * math.pi * (n[:, None] * n[None, :] % SIDE) / SIDE
    cosine = np.cos(angle) / math.sqrt(SIDE)
    sine = np.sin(angle) / math.sqrt(SIDE)
    first = np.block([[cosine, sine], [-sine, cosine]])
    high = first.astype(BF)
    low = (first - high.astype(np.float64)).astype(BF)
    return np.stack([high, low, high.T, low.T])


def sin_cos(value):
    turns = jnp.floor(value * (2.0 / math.pi) + 0.5)
    rest = value - turns * 1.5703125
    rest = rest - turns * 4.837512969970703125e-4
    rest = rest - turns * 7.54978995489188216e-8
    square = rest * rest
    sine = ((-1.9515295891e-4 * square + 8.3321608736e-3) * square - 1.6666654611e-1) * square * rest + rest
    cosine = ((2.443315711809948e-5 * square - 1.388731625493765e-3) * square + 4.166664568298827e-2) * square * square
    cosine = cosine - 0.5 * square + 1.0
    quadrant = turns.astype(jnp.int32)
    odd = (quadrant & 1) == 1
    flip_sine = (quadrant & 2) == 2
    flip_cosine = ((quadrant + 1) & 2) == 2
    s = jnp.where(odd, cosine, sine)
    c = jnp.where(odd, sine, cosine)
    return jnp.where(flip_sine, -s, s), jnp.where(flip_cosine, -c, c)


def dot(left, right):
    return jnp.dot(left, right, preferred_element_type=F32)


def halves(value):
    high = value.astype(BF)
    return high, (value - high.astype(F32)).astype(BF)


def kernel(
    offset_ref,
    count_ref,
    position_ref,
    volume_hbm,
    matrix_hbm,
    measured_hbm,
    probe_hbm,
    table_hbm,
    out_hbm,
    volume,
    matrix,
    measured,
    probe,
    table,
    matrices,
    offsets,
    tile_pad,
    grad_pad,
    s1,
    r1,
    acc1,
    s2,
    r2,
    acc2,
    s3,
    r3,
    sz,
    rz,
    full,
    window,
    t1,
    q1,
    t2,
    q2,
    t3,
    q3,
    zs,
    zr,
    slabs,
    out,
    load_sem,
    ssem,
    rsem,
):
    vx, y, s = lax.axis_index("vx"), lax.axis_index("vy"), lax.axis_index("scan")
    zl, x, c = vx // 8, (vx // 2) % 4, vx % 2

    def at(zl=zl, x=x, c=c, y=y, s=s):
        return (zl * 8 + x * 2 + c, y, s)

    def turn(index, d):
        return lax.rem(index + d, 4)

    def remote(number, src, dst, device):
        return pltpu.make_async_remote_copy(
            src_ref=src,
            dst_ref=dst,
            send_sem=ssem.at[number],
            recv_sem=rsem.at[number],
            device_id=device,
            device_id_type=MESH,
        )

    loads = [
        pltpu.make_async_copy(src, dst, load_sem.at[i])
        for i, (src, dst) in enumerate(
            [
                (volume_hbm, volume),
                (matrix_hbm, matrix),
                (measured_hbm, measured),
                (probe_hbm, probe),
                (table_hbm, table),
            ]
        )
    ]
    for load in loads:
        load.start()

    across = at(c=1 - c)
    partners = [across]
    partners += [at(x=turn(x, d)) for d in (1, 2, 3)]
    partners += [at(y=turn(y, d)) for d in (1, 2, 3)]
    column = [(dz, d) for dz in (0, 1) for d in range(4) if dz or d]
    partners += [at(zl=lax.rem(zl + dz, 2), s=turn(s, d)) for dz, d in column]
    barrier = pltpu.get_barrier_semaphore()
    for partner in partners:
        pl.semaphore_signal(barrier, inc=1, device_id=partner, device_id_type=MESH)

    for t in range(2):
        tile_pad[t, :, 0:384, :] = jnp.zeros((4, 384, 128), F32)
        tile_pad[t, :, 512:896, :] = jnp.zeros((4, 384, 128), F32)
    for k in range(CAP):
        grad_pad[k, :, 0:256, :] = jnp.zeros((4, 256, 128), F32)
        grad_pad[k, :, 512:768, :] = jnp.zeros((4, 256, 128), F32)
    for t in range(2):
        offsets[0, t] = jnp.full((8, 128), offset_ref[0, 0, t], jnp.int32)

    pl.semaphore_wait(barrier, len(partners))

    sent = []
    first_round = []
    for i, d in enumerate((1, 3)):
        for t in range(2):
            copy = remote(MATS + 2 * i + t, matrix_hbm.at[t], matrices.at[4 - d - 1, t], at(s=turn(s, d)))
            first_round.append(copy)
    for d in (1, 2, 3):
        copy = remote(OFFS + d - 1, offsets.at[0], offsets.at[4 - d], at(s=turn(s, d)))
        copy.start()
        sent.append(copy)

    loads[0].wait()
    loads[1].wait()
    for t in range(2):
        for part in range(2):
            block = volume[part, :, 32 * t : 32 * t + 32, :].reshape(1024, 256)
            shadow = lax.dot_general(
                matrix[t], block, (((0,), (0,)), ((), ())), preferred_element_type=F32
            )
            for j in range(2):
                tile_pad[t, 2 * part + j, 384:512, :] = shadow[:, 128 * j : 128 * j + 128]

    def placed(padded, starts, h):
        blocks = []
        for j in range(2):
            terms = [padded[i, 2 * h + j, pl.ds(start, 256), :] for i, start in enumerate(starts)]
            blocks.append(functools.reduce(jnp.add, terms))
        return jnp.concatenate(blocks, axis=1).reshape(4, 4, 16, 256)

    def placed_tiles(h, first):
        return placed(tile_pad, [384 - offset_ref[0, 0, t] + first for t in range(2)], h)

    def reduced(source, s1, r1, core_number, s2, r2, s3, r3, numbers, wire):
        for h in range(2):
            s1[h] = source(h, (1 - c) * 256).astype(wire)
        copy = remote(core_number, s1, r1, across)
        copy.start()
        sent.append(copy)
        for h in range(2):
            acc1[h] = source(h, c * 256)
        copy.wait_recv()
        copies = [[], []]
        for h in range(2):
            value = acc1[h] + r1[h].astype(F32)
            acc1[h] = value
            s2[h] = value.astype(wire)
            for d in (1, 2, 3):
                if h == 0:
                    to = turn(x, d)
                    copy = remote(numbers + d - 1, s2.at[0, to], r2.at[0, d - 1], at(x=to))
                else:
                    to = turn(y, d)
                    copy = remote(numbers + 3 + d - 1, s2.at[1, :, to], r2.at[1, d - 1], at(y=to))
                copy.start()
                sent.append(copy)
                copies[h].append(copy)
        later = [[], []]
        for h in range(2):
            value = acc1[0, x] if h == 0 else acc1[1, :, y]
            for d in (1, 2, 3):
                copies[h][d - 1].wait_recv()
            for d in (1, 2, 3):
                value = value + r2[h, d - 1].astype(F32)
            acc2[h] = value
            s3[h] = value.astype(wire)
            for d in (1, 2, 3):
                to = turn(y if h == 0 else x, d)
                device = at(y=to) if h == 0 else at(x=to)
                copy = remote(numbers + 6 + 3 * h + d - 1, s3.at[h, to], r3.at[h, d - 1], device)
                copy.start()
                sent.append(copy)
                later[h].append(copy)
        result = []
        for h in range(2):
            value = acc2[h, y if h == 0 else x]
            for d in (1, 2, 3):
                later[h][d - 1].wait_recv()
            for d in (1, 2, 3):
                value = value + r3[h, d - 1].astype(F32)
            result.append(value)
        return result

    def gathered(whole, n, numbers, core_number):
        copies = [[], []]
        for h in range(2):
            for d in (1, 2, 3):
                block = whole.at[pl.ds(n * h, n), c, x, y]
                device = at(y=turn(y, d)) if h == 0 else at(x=turn(x, d))
                copy = remote(numbers + 3 * h + d - 1, block, block, device)
                copy.start()
                sent.append(copy)
                copies[h].append(copy)
        later = []
        for h in range(2):
            for copy in copies[h]:
                copy.wait_recv()
            for d in (1, 2, 3):
                block = whole.at[pl.ds(0, n), c, x] if h == 0 else whole.at[pl.ds(n, n), c, :, y]
                device = at(x=turn(x, d)) if h == 0 else at(y=turn(y, d))
                copy = remote(numbers + 6 + 3 * h + d - 1, block, block, device)
                copy.start()
                sent.append(copy)
                later.append(copy)
        for copy in later:
            copy.wait_recv()
        block = whole.at[:, c]
        copy = remote(core_number, block, block, across)
        copy.start()
        sent.append(copy)
        copy.wait_recv()

    block = reduced(placed_tiles, s1, r1, CORE_P, s2, r2, s3, r3, RS_P, PROJ_WIRE)
    for h in range(2):
        sz[h] = block[h].astype(sz.dtype)
    copy = remote(Z_P, sz, rz, at(zl=1 - zl))
    copy.start()
    sent.append(copy)
    copy.wait_recv()
    for h in range(2):
        full[h, c, x, y] = (block[h] + rz[h].astype(F32)).astype(full.dtype)
    for copy in first_round:
        copy.start()
    gathered(full, 1, AG_P, CORE_GP)
    for h in range(2):
        projection = full[h].reshape(512, 256).astype(F32)
        for j in range(2):
            window[h, j] = projection[:, 128 * j : 128 * j + 128]

    for load in loads[2:]:
        load.wait()
    lane = lax.broadcasted_iota(jnp.int32, (256, 128), 1)
    for k in range(CAP):
        rows = pl.ds(position_ref[0, 0, k, 0], 256)
        phase, loss = (
            jnp.concatenate([window[part, j, rows, :] for j in range(2)], axis=1) for part in range(2)
        )
        sine, cosine = sin_cos(phase)
        amplitude = jnp.exp(-ABSORPTION * loss)
        cosine, sine = amplitude * cosine, amplitude * sine
        exit_re = probe[0] * cosine - probe[1] * sine
        exit_im = probe[0] * sine + probe[1] * cosine

        def left(which, value):
            high, low = halves(value)
            return dot(table[which], high) + dot(table[which], low) + dot(table[which + 1], high)

        def right(value, which):
            high, low = halves(value)
            return dot(high, table[which]) + dot(low, table[which]) + dot(high, table[which + 1])

        half = left(0, jnp.concatenate([exit_re, exit_im], axis=0))
        far = right(jnp.concatenate([half[:256], half[256:]], axis=1), 2)
        far_re, far_im = far[:, :256], far[:, 256:]
        residue = 4.0 * (far_re * far_re + far_im * far_im - measured[k])
        back = left(2, jnp.concatenate([residue * far_re, residue * far_im], axis=0))
        grad = right(jnp.concatenate([back[:256], back[256:]], axis=1), 0)
        grad_re, grad_im = grad[:, :256], grad[:, 256:]
        live = k < count_ref[0, 0]
        by_phase = jnp.where(live, grad_im * exit_re - grad_re * exit_im, 0.0)
        by_loss = jnp.where(live, -ABSORPTION * (grad_re * exit_re + grad_im * exit_im), 0.0)
        for h in range(2):
            a, b = by_phase[:, 128 * h : 128 * h + 128], by_loss[:, 128 * h : 128 * h + 128]
            even = jnp.where(lane < 64, a, pltpu.roll(b, 64, 1))
            odd = jnp.where(lane < 64, pltpu.roll(a, 64, 1), b)
            grad_pad[k, 2 * h, 256:512, :] = even
            grad_pad[k, 2 * h + 1, 256:512, :] = odd

    def placed_patches(h, first):
        return placed(grad_pad, [256 - position_ref[0, 0, k, 0] + first for k in range(CAP)], h)

    for copy in first_round:
        copy.wait_recv()
    second_round = [
        remote(MATS + 4, matrices.at[2, 0], matrices.at[1, 0], at(s=turn(s, 1))),
        remote(MATS + 5, matrices.at[0, 1], matrices.at[1, 1], at(s=turn(s, 3))),
    ]
    for copy in second_round:
        copy.start()

    block = reduced(placed_patches, t1, q1, CORE_I, t2, q2, t3, q3, RS_I, IMAGE_WIRE)
    for h in range(2):
        for j in range(2):
            zs[2 * h + j] = block[h][:, 128 * j : 128 * j + 128].astype(zs.dtype)
    zr[0, 0] = zs[s]
    copies = []
    for i, (dz, d) in enumerate(column):
        to = turn(s, d)
        copy = remote(Z_I + i, zs.at[to], zr.at[dz, (4 - d) % 4], at(zl=lax.rem(zl + dz, 2), s=to))
        copy.start()
        copies.append(copy)
        sent.append(copy)
    for copy in copies:
        copy.wait_recv()
    for k in range(4):
        slabs[k, c, x, y] = (zr[0, k].astype(F32) + zr[1, k].astype(F32)).astype(BF)
    gathered(slabs, 2, AG_I, CORE_GI)

    for copy in sent[:3]:
        copy.wait_recv()
    columns = lax.broadcasted_iota(jnp.int32, (128, 512), 1) - lax.broadcasted_iota(jnp.int32, (128, 512), 0)
    windows = []
    for t in range(2):
        pieces = []
        for k in range(4):
            first = jnp.broadcast_to(offsets[k, t][0:1, 0:1], (128, 512))
            chosen = jnp.where(columns == first, 1.0, 0.0).astype(BF)
            pieces.append(dot(chosen, slabs[k].reshape(512, 128)).astype(BF))
        windows.append(jnp.concatenate(pieces, axis=0))
    for copy in second_round:
        copy.wait_recv()
    stores = []
    for t in range(2):
        weights = jnp.concatenate([matrix[t], matrices[0, t], matrices[1, t], matrices[2, t]], axis=1)
        slope = (-STEP_LENGTH * dot(weights, windows[t])).reshape(32, 32, 128)
        for part in range(2):
            out[part, :, 32 * t : 32 * t + 32, :] = slope[:, :, 64 * part : 64 * part + 64]
        cut = pl.ds(32 * t, 32)
        store = pltpu.make_async_copy(out.at[:, :, cut, :], out_hbm.at[:, :, cut, :], load_sem.at[5 + t])
        store.start()
        stores.append(store)
    for store in stores:
        store.wait()
    for copy in sent + first_round + second_round:
        copy.wait_send()


def per_device(volume, tile_matrix, tile_offset, patch_count, scan_position, measured, illumination):
    any_space = pl.BlockSpec(memory_space=pl.ANY)
    smem = pl.BlockSpec(memory_space=pltpu.SMEM)
    wire = lambda kind: [
        pltpu.VMEM((2, 4, 4, 16, 256), kind),
        pltpu.VMEM((2, 4, 4, 16, 256), kind),
    ]
    return pl.pallas_call(
        kernel,
        out_shape=jax.ShapeDtypeStruct((2, 32, 64, 64), F32),
        in_specs=[smem] * 3 + [any_space] * 5,
        out_specs=any_space,
        scratch_shapes=[
            pltpu.VMEM((2, 32, 64, 256), BF),
            pltpu.VMEM((2, 1024, 128), BF),
            pltpu.VMEM((3, 256, 256), F32),
            pltpu.VMEM((2, 256, 256), F32),
            pltpu.VMEM((4, 512, 512), BF),
            pltpu.VMEM((3, 2, 1024, 128), BF),
            pltpu.VMEM((4, 2, 8, 128), jnp.int32),
            pltpu.VMEM((2, 4, 896, 128), F32),
            pltpu.VMEM((3, 4, 768, 128), F32),
            *wire(PROJ_WIRE),
            pltpu.VMEM((2, 4, 4, 16, 256), F32),
            pltpu.VMEM((2, 4, 4, 16, 256), PROJ_WIRE),
            pltpu.VMEM((2, 3, 4, 16, 256), PROJ_WIRE),
            pltpu.VMEM((2, 4, 16, 256), F32),
            pltpu.VMEM((2, 4, 16, 256), PROJ_WIRE),
            pltpu.VMEM((2, 3, 16, 256), PROJ_WIRE),
            pltpu.VMEM((2, 16, 256), F32),
            pltpu.VMEM((2, 16, 256), F32),
            pltpu.VMEM((2, 2, 4, 4, 16, 256), PROJ_FULL),
            pltpu.VMEM((2, 2, 512, 128), F32),
            *wire(IMAGE_WIRE),
            pltpu.VMEM((2, 4, 4, 16, 256), IMAGE_WIRE),
            pltpu.VMEM((2, 3, 4, 16, 256), IMAGE_WIRE),
            pltpu.VMEM((2, 4, 16, 256), IMAGE_WIRE),
            pltpu.VMEM((2, 3, 16, 256), IMAGE_WIRE),
            pltpu.VMEM((4, 16, 128), F32),
            pltpu.VMEM((2, 4, 16, 128), F32),
            pltpu.VMEM((4, 2, 4, 4, 16, 128), BF),
            pltpu.VMEM((2, 32, 64, 64), F32),
            pltpu.SemaphoreType.DMA((7,)),
            pltpu.SemaphoreType.DMA((N_SEMS,)),
            pltpu.SemaphoreType.DMA((N_SEMS,)),
        ],
        compiler_params=pltpu.CompilerParams(
            collective_id=0, has_side_effects=True, vmem_limit_bytes=60 * 2**20
        ),
    )(
        tile_offset,
        patch_count,
        scan_position,
        volume,
        tile_matrix.reshape(2, 1024, 128),
        measured.reshape(3, 256, 256),
        illumination,
        jnp.asarray(tables()),
    )


def solution(mesh):
    in_specs = (
        P(None, "vx", "vy", None),
        P("scan", "vx", "vy", None, None),
        P("scan", "vx", "vy"),
        P("scan", ("vx", "vy")),
        P("scan", ("vx", "vy"), None, None),
        P("scan", ("vx", "vy"), None, None, None),
        P(),
    )
    out_specs = P(None, "vx", "vy", "scan")
    return jax.shard_map(
        per_device, mesh=mesh, in_specs=in_specs, out_specs=out_specs, check_vma=False
    )
```

profile of v0, /device:TPU:1, one launch (start us, length us, event | category | flops | bytes accessed | tf_op | source)
XLA Modules:
  0.0 80.4 jit_solution(5491716289372548550)
XLA Ops:
  0.7 1.3 %copy.9.position_ref = s32[1,1,3,2]{3,2,1,0:T(4,128)} copy(s32[1,1,3,2]{2,3,1,0:T(2,128)} %param.12) | data formatting | bytes 48 | tf_op args[4]
  2.0 75.3 %shard_map.82 = f32[2,32,64,64]{3,2,1,0:T(8,128)} custom-call(s32[1,1,2]{2,1,0:T(1,128)} %offset_ref.1, s32[1,1]{1,0:T(1,128)S(6)} %copy.11.count_ref, s32[1,1,3,2]{3,2,1,0:T(4,128)} %copy.9.position_ref, bf16[2,32,64,256]{3,2,1,0:T(8,128)(2,1)} %volume_hbm.1, bf16[2,1024,128]{2,1,0:T(8,128)(2,1)} %bitcast.3, f32[3,256,256]{2,1,0:T(8,128)} %bitcast.2, ...), custom_call_target="tpu_custom_call" | custom-call | tf_op jit(solution)/shard_map/pallas_call | solution.py:407
  77.3 3.2 %copy.12 = f32[2,32,64,64]{3,2,1,0:T(8,128)} copy(f32[2,32,64,64]{3,2,1,0:T(8,128)} %shard_map.82) | data formatting | bytes 2097152
where the time goes:
time: 80.6 us; the launch traced here: 80.4 us
  Pallas kernels  75.3 us (93%)
  local copies, waits for them, and re-layouts  4.5 us (6%)
    pallas_call x1, Pallas kernels, per_device(): pl.pallas_call(kernel, out_shape=jax.ShapeDtypeStruct((2, 32, 64, 64), F3...  75.3 us
    unnamed x2, local copies, waits for them, and re-layouts  4.5 us

commit v1 on v0

v1 whole, which is shorter than its diff:
```python
import functools
import math

import jax
import jax.numpy as jnp
import numpy as np
from jax import lax
from jax.experimental import pallas as pl
from jax.experimental.pallas import tpu as pltpu
from jax.sharding import PartitionSpec as P

MESH = pl.DeviceIdType.MESH
BF = jnp.bfloat16
F32 = jnp.float32

ABSORPTION = 0.2
STEP_LENGTH = 0.003
SIDE = 256
CAP = 3

CORE_P, CORE_I, Z_P, CORE_GP, CORE_GI = range(5)
MATS = 5
OFFS = 11
RS_P, RS_I, AG_P, AG_I = 14, 29, 44, 59
Z_I = 74
N_SEMS = 81

PLANE = sorted(
    ((dx, dy) for dx in range(4) for dy in range(4) if dx or dy),
    key=lambda step: -sum(min(d, 4 - d) for d in step),
)
COLUMN = [(dz, d) for d in (2, 1, 3, 0) for dz in (1, 0) if dz or d]


def tables():
    n = np.arange(SIDE)
    angle = 2.0 * math.pi * (n[:, None] * n[None, :] % SIDE) / SIDE
    cosine = np.cos(angle) / math.sqrt(SIDE)
    sine = np.sin(angle) / math.sqrt(SIDE)
    first = np.block([[cosine, sine], [-sine, cosine]])
    return np.stack([first, first.T]).astype(BF)


def sin_cos(value):
    turns = jnp.floor(value * (2.0 / math.pi) + 0.5)
    rest = value - turns * 1.5703125
    rest = rest - turns * 4.837512969970703125e-4
    rest = rest - turns * 7.54978995489188216e-8
    square = rest * rest
    sine = ((-1.9515295891e-4 * square + 8.3321608736e-3) * square - 1.6666654611e-1) * square * rest + rest
    cosine = ((2.443315711809948e-5 * square - 1.388731625493765e-3) * square + 4.166664568298827e-2) * square * square
    cosine = cosine - 0.5 * square + 1.0
    quadrant = turns.astype(jnp.int32)
    odd = (quadrant & 1) == 1
    flip_sine = (quadrant & 2) == 2
    flip_cosine = ((quadrant + 1) & 2) == 2
    s = jnp.where(odd, cosine, sine)
    c = jnp.where(odd, sine, cosine)
    return jnp.where(flip_sine, -s, s), jnp.where(flip_cosine, -c, c)


def dot(left, right):
    return jnp.dot(left, right, preferred_element_type=F32)


def kernel(
    offset_ref,
    count_ref,
    position_ref,
    volume_hbm,
    matrix_hbm,
    measured_hbm,
    probe_hbm,
    table_hbm,
    windows_out,
    matrices,
    volume,
    matrix,
    measured,
    probe,
    table,
    offsets,
    tile_pad,
    grad_pad,
    s1,
    r1,
    acc1,
    s2,
    r2,
    sz,
    rz,
    full,
    window,
    t1,
    q1,
    acc2,
    t2,
    q2,
    zs,
    zr,
    slabs,
    load_sem,
    ssem,
    rsem,
):
    vx, y, s = lax.axis_index("vx"), lax.axis_index("vy"), lax.axis_index("scan")
    zl, x, c = vx // 8, (vx // 2) % 4, vx % 2

    def at(zl=zl, x=x, c=c, y=y, s=s):
        return (zl * 8 + x * 2 + c, y, s)

    def turn(index, d):
        return lax.rem(index + d, 4)

    def remote(number, src, dst, device):
        return pltpu.make_async_remote_copy(
            src_ref=src,
            dst_ref=dst,
            send_sem=ssem.at[number],
            recv_sem=rsem.at[number],
            device_id=device,
            device_id_type=MESH,
        )

    loads = [
        pltpu.make_async_copy(src, dst, load_sem.at[i])
        for i, (src, dst) in enumerate(
            [
                (volume_hbm, volume),
                (matrix_hbm, matrix),
                (measured_hbm, measured),
                (probe_hbm, probe),
                (table_hbm, table),
            ]
        )
    ]
    for load in loads:
        load.start()

    across = at(c=1 - c)
    plane = [at(x=turn(x, dx), y=turn(y, dy)) for dx, dy in PLANE]
    column = [at(zl=lax.rem(zl + dz, 2), s=turn(s, d)) for dz, d in COLUMN]
    barrier = pltpu.get_barrier_semaphore()
    for partner in [*column, *plane, across]:
        pl.semaphore_signal(barrier, inc=1, device_id=partner, device_id_type=MESH)

    for t in range(2):
        tile_pad[t, :, 0:384, :] = jnp.zeros((4, 384, 128), F32)
        tile_pad[t, :, 512:896, :] = jnp.zeros((4, 384, 128), F32)
    for k in range(CAP):
        grad_pad[k, :, 0:256, :] = jnp.zeros((4, 256, 128), F32)
        grad_pad[k, :, 512:768, :] = jnp.zeros((4, 256, 128), F32)
    for t in range(2):
        offsets[0, t] = jnp.full((8, 128), offset_ref[0, 0, t], jnp.int32)

    loads[0].wait()
    loads[1].wait()
    for t in range(2):
        for part in range(2):
            block = volume[part, :, 32 * t : 32 * t + 32, :].reshape(1024, 256)
            shadow = lax.dot_general(
                matrix[t], block, (((0,), (0,)), ((), ())), preferred_element_type=F32
            )
            for j in range(2):
                tile_pad[t, 2 * part + j, 384:512, :] = shadow[:, 128 * j : 128 * j + 128]

    def placed(padded, starts, h):
        blocks = []
        for j in range(2):
            terms = [padded[i, 2 * h + j, pl.ds(start, 256), :] for i, start in enumerate(starts)]
            blocks.append(functools.reduce(jnp.add, terms))
        return jnp.concatenate(blocks, axis=1).reshape(4, 4, 16, 256)

    def placed_tiles(h, first):
        return placed(tile_pad, [384 - offset_ref[0, 0, t] + first for t in range(2)], h)

    def reduced(source, s1, r1, core_number, acc, s2, r2, numbers):
        copy = remote(core_number, s1, r1, across)
        copy.start()
        sent.append(copy)
        for h in range(2):
            acc[:, :, h] = source(h, c * 256)
        copy.wait_recv()
        value = acc[...] + r1[...].astype(F32)
        acc[...] = value
        s2[...] = value.astype(BF)
        copies = []
        for i, (dx, dy) in enumerate(PLANE):
            copy = remote(numbers + i, s2.at[turn(x, dx), turn(y, dy)], r2.at[i], plane[i])
            copy.start()
            copies.append(copy)
        sent.extend(copies)
        value = acc[x, y]
        for copy in copies:
            copy.wait_recv()
        for i in range(len(PLANE)):
            value = value + r2[i].astype(F32)
        return value

    def gathered(whole, numbers, core_number):
        copies = []
        block = whole.at[c, x, y]
        for i in range(len(PLANE)):
            copy = remote(numbers + i, block, block, plane[i])
            copy.start()
            copies.append(copy)
        sent.extend(copies)
        for copy in copies:
            copy.wait_recv()
        block = whole.at[c]
        copy = remote(core_number, block, block, across)
        copy.start()
        sent.append(copy)
        copy.wait_recv()

    for h in range(2):
        s1[:, :, h] = placed_tiles(h, (1 - c) * 256).astype(BF)

    pl.semaphore_wait(barrier, 1 + len(PLANE) + len(COLUMN))
    sent = []
    first_round = []
    for i, d in enumerate((1, 3)):
        for t in range(2):
            copy = remote(MATS + 2 * i + t, matrix_hbm.at[t], matrices.at[3 - d, t], at(s=turn(s, d)))
            first_round.append(copy)
    early = []
    for d in (1, 2, 3):
        copy = remote(OFFS + d - 1, offsets.at[0], offsets.at[4 - d], at(s=turn(s, d)))
        early.append(copy)

    for copy in early:
        copy.start()
    for copy in (first_round[0], first_round[3]):
        copy.start()
    block = reduced(placed_tiles, s1, r1, CORE_P, acc1, s2, r2, RS_P)
    sz[...] = block
    copy = remote(Z_P, sz, rz, at(zl=1 - zl))
    copy.start()
    sent.append(copy)
    copy.wait_recv()
    for copy in (first_round[0], first_round[3]):
        copy.wait_recv()
    second_round = [
        remote(MATS + 4, matrices.at[2, 0], matrices.at[1, 0], at(s=turn(s, 1))),
        remote(MATS + 5, matrices.at[0, 1], matrices.at[1, 1], at(s=turn(s, 3))),
    ]
    for copy in second_round:
        copy.start()
    for copy in first_round[1:3]:
        copy.start()
    full[c, x, y] = (block + rz[...]).astype(BF)
    gathered(full, AG_P, CORE_GP)
    for h in range(2):
        projection = full[:, :, :, h].reshape(512, 256).astype(F32)
        for j in range(2):
            window[h, j] = projection[:, 128 * j : 128 * j + 128]

    for load in loads[2:]:
        load.wait()
    lane = lax.broadcasted_iota(jnp.int32, (256, 128), 1)
    for k in range(CAP):
        rows = pl.ds(position_ref[0, 0, 0, k], 256)
        phase, loss = (
            jnp.concatenate([window[part, j, rows, :] for j in range(2)], axis=1) for part in range(2)
        )
        sine, cosine = sin_cos(phase)
        amplitude = jnp.exp(-ABSORPTION * loss)
        cosine, sine = amplitude * cosine, amplitude * sine
        exit_re = probe[0] * cosine - probe[1] * sine
        exit_im = probe[0] * sine + probe[1] * cosine

        half = dot(table[0], jnp.concatenate([exit_re, exit_im], axis=0).astype(BF)).astype(BF)
        far = dot(jnp.concatenate([half[:256], half[256:]], axis=1), table[1])
        far_re, far_im = far[:, :256], far[:, 256:]
        residue = 4.0 * (far_re * far_re + far_im * far_im - measured[k])
        residue_far = jnp.concatenate([residue * far_re, residue * far_im], axis=0).astype(BF)
        back = dot(table[1], residue_far).astype(BF)
        grad = dot(jnp.concatenate([back[:256], back[256:]], axis=1), table[0])
        grad_re, grad_im = grad[:, :256], grad[:, 256:]
        live = k < count_ref[0, 0]
        by_phase = jnp.where(live, grad_im * exit_re - grad_re * exit_im, 0.0)
        by_loss = jnp.where(live, -ABSORPTION * (grad_re * exit_re + grad_im * exit_im), 0.0)
        for h in range(2):
            a, b = by_phase[:, 128 * h : 128 * h + 128], by_loss[:, 128 * h : 128 * h + 128]
            even = jnp.where(lane < 64, a, pltpu.roll(b, 64, 1))
            odd = jnp.where(lane < 64, pltpu.roll(a, 64, 1), b)
            grad_pad[k, 2 * h, 256:512, :] = even
            grad_pad[k, 2 * h + 1, 256:512, :] = odd

    def placed_patches(h, first):
        return placed(grad_pad, [256 - position_ref[0, 0, 0, k] + first for k in range(CAP)], h)

    for h in range(2):
        t1[:, :, h] = placed_patches(h, (1 - c) * 256).astype(BF)
    block = reduced(placed_patches, t1, q1, CORE_I, acc2, t2, q2, RS_I)
    for k in range(4):
        zs[k] = block[k // 2, :, 128 * (k % 2) : 128 * (k % 2) + 128]
    zr[0, 0] = zs[s]
    copies = []
    for i, (dz, d) in enumerate(COLUMN):
        copy = remote(Z_I + i, zs.at[turn(s, d)], zr.at[dz, (4 - d) % 4], column[i])
        copy.start()
        copies.append(copy)
    sent.extend(copies)
    for copy in copies:
        copy.wait_recv()
    slabs[c, x, y] = (zr[0] + zr[1]).astype(BF)
    gathered(slabs, AG_I, CORE_GI)

    for copy in early:
        copy.wait_recv()
    columns = lax.broadcasted_iota(jnp.int32, (128, 512), 1) - lax.broadcasted_iota(jnp.int32, (128, 512), 0)
    for k in range(4):
        slab = slabs[:, :, :, k].reshape(512, 128)
        for t in range(2):
            first = jnp.broadcast_to(offsets[k, t][0:1, 0:1], (128, 512))
            chosen = jnp.where(columns == first, 1.0, 0.0).astype(BF)
            windows_out[t, 128 * k : 128 * k + 128, :] = dot(chosen, slab).astype(BF)
    for copy in first_round[1:3] + second_round:
        copy.wait_recv()
    for copy in sent + early + first_round + second_round:
        copy.wait_send()


def back_kernel(windows, own_hbm, matrices_hbm, out_hbm, weights, out, load_sem, store_sem):
    loads = []
    for t in range(2):
        for k in range(4):
            source = own_hbm.at[t] if k == 0 else matrices_hbm.at[k - 1, t]
            load = pltpu.make_async_copy(source, weights.at[t, k], load_sem.at[t, k])
            load.start()
            loads.append(load)
    stores = []
    for t in range(2):
        for k in range(4):
            loads[4 * t + k].wait()
        side = jnp.concatenate([weights[t, k] for k in range(4)], axis=1)
        slope = (-STEP_LENGTH * dot(side, windows[t])).reshape(32, 32, 128)
        for part in range(2):
            out[part, :, 32 * t : 32 * t + 32, :] = slope[:, :, 64 * part : 64 * part + 64]
        cut = pl.ds(32 * t, 32)
        store = pltpu.make_async_copy(out.at[:, :, cut, :], out_hbm.at[:, :, cut, :], store_sem.at[t])
        store.start()
        stores.append(store)
    for store in stores:
        store.wait()


def per_device(volume, tile_matrix, tile_offset, patch_count, scan_position, measured, illumination):
    any_space = pl.BlockSpec(memory_space=pl.ANY)
    smem = pl.BlockSpec(memory_space=pltpu.SMEM)
    block = (4, 4, 2, 16, 256)
    tile_matrix = tile_matrix.reshape(2, 1024, 128)
    windows, matrices = pl.pallas_call(
        kernel,
        out_shape=(
            jax.ShapeDtypeStruct((2, 512, 128), BF),
            jax.ShapeDtypeStruct((3, 2, 1024, 128), BF),
        ),
        in_specs=[smem] * 3 + [any_space] * 5,
        out_specs=(pl.BlockSpec(memory_space=pltpu.VMEM), any_space),
        scratch_shapes=[
            pltpu.VMEM((2, 32, 64, 256), BF),
            pltpu.VMEM((2, 1024, 128), BF),
            pltpu.VMEM((3, 256, 256), F32),
            pltpu.VMEM((2, 256, 256), F32),
            pltpu.VMEM((2, 512, 512), BF),
            pltpu.VMEM((4, 2, 8, 128), jnp.int32),
            pltpu.VMEM((2, 4, 896, 128), F32),
            pltpu.VMEM((3, 4, 768, 128), F32),
            pltpu.VMEM(block, BF),
            pltpu.VMEM(block, BF),
            pltpu.VMEM(block, F32),
            pltpu.VMEM(block, BF),
            pltpu.VMEM((15, 2, 16, 256), BF),
            pltpu.VMEM((2, 16, 256), F32),
            pltpu.VMEM((2, 16, 256), F32),
            pltpu.VMEM((2, *block), BF),
            pltpu.VMEM((2, 2, 512, 128), F32),
            pltpu.VMEM(block, BF),
            pltpu.VMEM(block, BF),
            pltpu.VMEM(block, F32),
            pltpu.VMEM(block, BF),
            pltpu.VMEM((15, 2, 16, 256), BF),
            pltpu.VMEM((4, 16, 128), F32),
            pltpu.VMEM((2, 4, 16, 128), F32),
            pltpu.VMEM((2, 4, 4, 4, 16, 128), BF),
            pltpu.SemaphoreType.DMA((5,)),
            pltpu.SemaphoreType.DMA((N_SEMS,)),
            pltpu.SemaphoreType.DMA((N_SEMS,)),
        ],
        compiler_params=pltpu.CompilerParams(
            collective_id=0, has_side_effects=True, vmem_limit_bytes=60 * 2**20
        ),
    )(
        tile_offset,
        patch_count,
        jnp.swapaxes(scan_position, 2, 3),
        volume,
        tile_matrix,
        measured.reshape(3, 256, 256),
        illumination,
        jnp.asarray(tables()),
    )
    return pl.pallas_call(
        back_kernel,
        out_shape=jax.ShapeDtypeStruct((2, 32, 64, 64), F32),
        in_specs=[pl.BlockSpec(memory_space=pltpu.VMEM), any_space, any_space],
        out_specs=any_space,
        scratch_shapes=[
            pltpu.VMEM((2, 4, 1024, 128), BF),
            pltpu.VMEM((2, 32, 64, 64), F32),
            pltpu.SemaphoreType.DMA((2, 4)),
            pltpu.SemaphoreType.DMA((2,)),
        ],
        compiler_params=pltpu.CompilerParams(vmem_limit_bytes=60 * 2**20),
    )(windows, tile_matrix, matrices)


def solution(mesh):
    in_specs = (
        P(None, "vx", "vy", None),
        P("scan", "vx", "vy", None, None),
        P("scan", "vx", "vy"),
        P("scan", ("vx", "vy")),
        P("scan", ("vx", "vy"), None, None),
        P("scan", ("vx", "vy"), None, None, None),
        P(),
    )
    out_specs = P(None, "vx", "vy", "scan")
    return jax.shard_map(
        per_device, mesh=mesh, in_specs=in_specs, out_specs=out_specs, check_vma=False
    )
```

time: 80.6 us -> 68 us (0.84)
  Pallas kernels: 75.3 us -> 67.2 us
  local copies, waits for them, and re-layouts: 4.5 us -> 0 us
    pallas_call x1 -> x2, Pallas kernels: 75.3 us -> 67.2 us  [the longest x1 62.4 us: per_device(): pl.pallas_call(kernel, out_shape=(jax.ShapeDtypeStruct((2, 512, 128), BF)...]
    unnamed x2 -> x0, local copies, waits for them, and re-layouts: 4.5 us -> none
where the time goes in v1:
time: 68 us; the launch traced here: 67.8 us
  Pallas kernels  67.2 us (99%)
    pallas_call x1, Pallas kernels, per_device(): pl.pallas_call(kernel, out_shape=(jax.ShapeDtypeStruct((2, 512, 128), BF)...  62.4 us
    pallas_call x1, Pallas kernels, per_device(): pl.pallas_call(back_kernel, out_shape=jax.ShapeDtypeStruct((2, 32, 64, 64...  4.72 us

profile of v1, /device:TPU:1, one launch (start us, length us, event | category | flops | bytes accessed | tf_op | source)
XLA Modules:
  0.0 67.8 jit_solution(7674856282556674996)
XLA Ops:
  0.7 62.4 %shard_map.82 = (bf16[2,512,128]{2,1,0:T(8,128)(2,1)}, bf16[3,2,1024,128]{3,2,1,0:T(8,128)(2,1)}) custom-call(s32[1,1,2]{2,1,0:T(1,128)} %offset_ref.1, s32[1,1]{1,0:T(1,128)S(6)} %copy.9.count_ref, s32[1,1,2,3]{3,2,1,0:T(2,128)} %bitcast.6, bf16[2,32,64,256]{3,2,1,0:T(8,128)(2,1)} %volume_hbm.1, bf16[2,1024,128]{2,1,0:T(8,128)(2,1)} %bitcast.3, ...), custom_call_target="tpu_custom_call" | custom-call | tf_op jit(solution)/shard_map/pallas_call | solution.py:354
  63.1 4.7 %shard_map.83 = f32[2,32,64,64]{3,2,1,0:T(8,128)} custom-call(bf16[2,512,128]{2,1,0:T(8,128)(2,1)} %get-tuple-element.7.windows, bf16[2,1024,128]{2,1,0:T(8,128)(2,1)} %bitcast.4, bf16[3,2,1024,128]{3,2,1,0:T(8,128)(2,1)} %get-tuple-element.8.matrices_hbm), custom_call_target="tpu_custom_call" | custom-call | tf_op jit(solution)/shard_map/pallas_call | solution.py:405

commit v2 on v1

--- a/solution.py
+++ b/solution.py
@@ -19,11 +19,13 @@
 CAP = 3
 
 CORE_P, CORE_I, Z_P, CORE_GP, CORE_GI = range(5)
-MATS = 5
-OFFS = 11
-RS_P, RS_I, AG_P, AG_I = 14, 29, 44, 59
-Z_I = 74
-N_SEMS = 81
+OFFS = 5
+RS_P, RS_I, AG_P, AG_I = 8, 23, 38, 53
+Z_I = 68
+MATS = 75
+N_SEMS = 99
+
+BEFORE, BETWEEN = (0, 1), (2, 3, 4, 5, 8, 9)
 
 PLANE = sorted(
     ((dx, dy) for dx in range(4) for dy in range(4) if dx or dy),
@@ -218,11 +220,27 @@
 
     pl.semaphore_wait(barrier, 1 + len(PLANE) + len(COLUMN))
     sent = []
-    first_round = []
-    for i, d in enumerate((1, 3)):
-        for t in range(2):
-            copy = remote(MATS + 2 * i + t, matrix_hbm.at[t], matrices.at[3 - d, t], at(s=turn(s, d)))
-            first_round.append(copy)
+    right, left = at(s=turn(s, 1)), at(s=turn(s, 3))
+    steps = []
+    for i in range(12):
+        t, quarter = (0, 0, 1)[i // 4], pl.ds(256 * (i % 4), 256)
+        for j, device in enumerate((right, left)):
+            tile = t if j == 0 else 1 - t
+            own = matrix_hbm.at[tile, quarter]
+            there = matrices.at[2 - 2 * j, tile, quarter]
+            if i // 4 == 1:
+                own, there = there, matrices.at[1, tile, quarter]
+            steps.append(remote(MATS + 2 * i + j, own, there, device))
+    arrived = set()
+
+    def go(wanted):
+        for i in wanted:
+            for j in range(2):
+                if i // 4 == 1:
+                    steps[2 * (i - 4) + j].wait_recv()
+                    arrived.add(2 * (i - 4) + j)
+                steps[2 * i + j].start()
+
     early = []
     for d in (1, 2, 3):
         copy = remote(OFFS + d - 1, offsets.at[0], offsets.at[4 - d], at(s=turn(s, d)))
@@ -230,24 +248,14 @@
 
     for copy in early:
         copy.start()
-    for copy in (first_round[0], first_round[3]):
-        copy.start()
+    go(BEFORE)
     block = reduced(placed_tiles, s1, r1, CORE_P, acc1, s2, r2, RS_P)
     sz[...] = block
     copy = remote(Z_P, sz, rz, at(zl=1 - zl))
     copy.start()
     sent.append(copy)
     copy.wait_recv()
-    for copy in (first_round[0], first_round[3]):
-        copy.wait_recv()
-    second_round = [
-        remote(MATS + 4, matrices.at[2, 0], matrices.at[1, 0], at(s=turn(s, 1))),
-        remote(MATS + 5, matrices.at[0, 1], matrices.at[1, 1], at(s=turn(s, 3))),
-    ]
-    for copy in second_round:
-        copy.start()
-    for copy in first_round[1:3]:
-        copy.start()
+    go(BETWEEN)
     full[c, x, y] = (block + rz[...]).astype(BF)
     gathered(full, AG_P, CORE_GP)
     for h in range(2):
@@ -304,6 +312,7 @@
     sent.extend(copies)
     for copy in copies:
         copy.wait_recv()
+    go([i for i in range(12) if i not in BEFORE and i not in BETWEEN])
     slabs[c, x, y] = (zr[0] + zr[1]).astype(BF)
     gathered(slabs, AG_I, CORE_GI)
 
@@ -316,32 +325,38 @@
             first = jnp.broadcast_to(offsets[k, t][0:1, 0:1], (128, 512))
             chosen = jnp.where(columns == first, 1.0, 0.0).astype(BF)
             windows_out[t, 128 * k : 128 * k + 128, :] = dot(chosen, slab).astype(BF)
-    for copy in first_round[1:3] + second_round:
-        copy.wait_recv()
-    for copy in sent + early + first_round + second_round:
+    for i, copy in enumerate(steps):
+        if i not in arrived:
+            copy.wait_recv()
+    for copy in sent + early + steps:
         copy.wait_send()
 
 
-def back_kernel(windows, own_hbm, matrices_hbm, out_hbm, weights, out, load_sem, store_sem):
-    loads = []
+def back_kernel(windows_hbm, own_hbm, matrices_hbm, out_hbm, windows, weights, out, load_sem, store_sem):
+    loads = [pltpu.make_async_copy(windows_hbm, windows, load_sem.at[4])]
     for t in range(2):
-        for k in range(4):
-            source = own_hbm.at[t] if k == 0 else matrices_hbm.at[k - 1, t]
-            load = pltpu.make_async_copy(source, weights.at[t, k], load_sem.at[t, k])
-            load.start()
-            loads.append(load)
+        loads += [
+            pltpu.make_async_copy(own_hbm.at[t], weights.at[t, 0], load_sem.at[2 * t]),
+            pltpu.make_async_copy(matrices_hbm.at[:, t], weights.at[t, pl.ds(1, 3)], load_sem.at[2 * t + 1]),
+        ]
+    for load in loads:
+        load.start()
+    for load in loads:
+        load.wait()
     stores = []
-    for t in range(2):
-        for k in range(4):
-            loads[4 * t + k].wait()
-        side = jnp.concatenate([weights[t, k] for k in range(4)], axis=1)
-        slope = (-STEP_LENGTH * dot(side, windows[t])).reshape(32, 32, 128)
+    for quarter in range(4):
+        lines = pl.ds(8 * quarter, 8)
+        for t in range(2):
+            side = jnp.concatenate([weights[t, k, 256 * quarter : 256 * quarter + 256] for k in range(4)], axis=1)
+            slope = (-STEP_LENGTH * dot(side, windows[t])).reshape(8, 32, 128)
+            for part in range(2):
+                out[part, lines, 32 * t : 32 * t + 32, :] = slope[:, :, 64 * part : 64 * part + 64]
         for part in range(2):
-            out[part, :, 32 * t : 32 * t + 32, :] = slope[:, :, 64 * part : 64 * part + 64]
-        cut = pl.ds(32 * t, 32)
-        store = pltpu.make_async_copy(out.at[:, :, cut, :], out_hbm.at[:, :, cut, :], store_sem.at[t])
-        store.start()
-        stores.append(store)
+            store = pltpu.make_async_copy(
+                out.at[part, lines], out_hbm.at[part, lines], store_sem.at[2 * quarter + part]
+            )
+            store.start()
+            stores.append(store)
     for store in stores:
         store.wait()
 
@@ -405,13 +420,14 @@
     return pl.pallas_call(
         back_kernel,
         out_shape=jax.ShapeDtypeStruct((2, 32, 64, 64), F32),
-        in_specs=[pl.BlockSpec(memory_space=pltpu.VMEM), any_space, any_space],
+        in_specs=[any_space] * 3,
         out_specs=any_space,
         scratch_shapes=[
+            pltpu.VMEM((2, 512, 128), BF),
             pltpu.VMEM((2, 4, 1024, 128), BF),
             pltpu.VMEM((2, 32, 64, 64), F32),
-            pltpu.SemaphoreType.DMA((2, 4)),
-            pltpu.SemaphoreType.DMA((2,)),
+            pltpu.SemaphoreType.DMA((5,)),
+            pltpu.SemaphoreType.DMA((8,)),
         ],
         compiler_params=pltpu.CompilerParams(vmem_limit_bytes=60 * 2**20),
     )(windows, tile_matrix, matrices)

time: 68 us -> 61.7 us (0.907)
  Pallas kernels: 67.2 us -> 60.2 us
    pallas_call x1, Pallas kernels: 62.4 us -> 56.9 us  [per_device(): pl.pallas_call(kernel, out_shape=(jax.ShapeDtypeStruct((2, 512, 128), BF)...]
    pallas_call x1, Pallas kernels: 4.72 us -> 3.39 us  [per_device(): pl.pallas_call(back_kernel, out_shape=jax.ShapeDtypeStruct((2, 32, 64, 64...]
where the time goes in v2:
time: 61.7 us; the launch traced here: 60.9 us
  Pallas kernels  60.2 us (98%)
  between operations  0.66 us (1%)
    pallas_call x1, Pallas kernels, per_device(): pl.pallas_call(kernel, out_shape=(jax.ShapeDtypeStruct((2, 512, 128), BF)...  56.9 us
    pallas_call x1, Pallas kernels, per_device(): pl.pallas_call(back_kernel, out_shape=jax.ShapeDtypeStruct((2, 32, 64, 64...  3.39 us

profile of v2, /device:TPU:1, one launch (start us, length us, event | category | flops | bytes accessed | tf_op | source)
XLA Modules:
  0.0 60.9 jit_solution(17965479819008492099)
XLA Ops:
  0.7 56.9 %shard_map.82 = (bf16[2,512,128]{2,1,0:T(8,128)(2,1)}, bf16[3,2,1024,128]{3,2,1,0:T(8,128)(2,1)}) custom-call(s32[1,1,2]{2,1,0:T(1,128)} %offset_ref.1, s32[1,1]{1,0:T(1,128)S(6)} %copy.9.count_ref, s32[1,1,2,3]{3,2,1,0:T(2,128)} %bitcast.6, bf16[2,32,64,256]{3,2,1,0:T(8,128)(2,1)} %volume_hbm.1, bf16[2,1024,128]{2,1,0:T(8,128)(2,1)} %bitcast.3, ...), custom_call_target="tpu_custom_call" | custom-call | tf_op jit(solution)/shard_map/pallas_call | solution.py:369
  57.5 3.4 %shard_map.83 = f32[2,32,64,64]{3,2,1,0:T(8,128)} custom-call(bf16[2,512,128]{2,1,0:T(8,128)(2,1)} %get-tuple-element.7.windows_hbm, bf16[2,1024,128]{2,1,0:T(8,128)(2,1)} %bitcast.4, bf16[3,2,1024,128]{3,2,1,0:T(8,128)(2,1)} %get-tuple-element.8.matrices_hbm), custom_call_target="tpu_custom_call" | custom-call | tf_op jit(solution)/shard_map/pallas_call | solution.py:420

commit v3 on v2

--- a/solution.py
+++ b/solution.py
@@ -18,19 +18,18 @@
 SIDE = 256
 CAP = 3
 
-CORE_P, CORE_I, Z_P, CORE_GP, CORE_GI = range(5)
-OFFS = 5
-RS_P, RS_I, AG_P, AG_I = 8, 23, 38, 53
-Z_I = 68
-MATS = 75
-N_SEMS = 99
+CORE_P, CORE_I, CORE_GP, CORE_GI = 0, 4, 8, 12
+Z_P = 16
+OFFS = 17
+RS_P, RS_I, AG_P, AG_I = 20, 35, 50, 65
+Z_I = 80
+MATS = 87
+N_SEMS = 111
 
 BEFORE, BETWEEN = (0, 1), (2, 3, 4, 5, 8, 9)
 
-PLANE = sorted(
-    ((dx, dy) for dx in range(4) for dy in range(4) if dx or dy),
-    key=lambda step: -sum(min(d, 4 - d) for d in step),
-)
+ROWS = (2, 1, 3, 0)
+PLANE = [(dx, dy) for dx in ROWS for dy in (2, 1, 3, 0) if dx or dy]
 COLUMN = [(dz, d) for d in (2, 1, 3, 0) for dz in (1, 0) if dz or d]
 
 
@@ -77,7 +76,6 @@
     windows_out,
     matrices,
     volume,
-    matrix,
     measured,
     probe,
     table,
@@ -101,6 +99,8 @@
     zs,
     zr,
     slabs,
+    picks,
+    own_rows,
     load_sem,
     ssem,
     rsem,
@@ -129,7 +129,7 @@
         for i, (src, dst) in enumerate(
             [
                 (volume_hbm, volume),
-                (matrix_hbm, matrix),
+                (matrix_hbm, matrices.at[0]),
                 (measured_hbm, measured),
                 (probe_hbm, probe),
                 (table_hbm, table),
@@ -161,7 +161,7 @@
         for part in range(2):
             block = volume[part, :, 32 * t : 32 * t + 32, :].reshape(1024, 256)
             shadow = lax.dot_general(
-                matrix[t], block, (((0,), (0,)), ((), ())), preferred_element_type=F32
+                matrices[0, t], block, (((0,), (0,)), ((), ())), preferred_element_type=F32
             )
             for j in range(2):
                 tile_pad[t, 2 * part + j, 384:512, :] = shadow[:, 128 * j : 128 * j + 128]
@@ -169,29 +169,44 @@
     def placed(padded, starts, h):
         blocks = []
         for j in range(2):
-            terms = [padded[i, 2 * h + j, pl.ds(start, 256), :] for i, start in enumerate(starts)]
+            terms = [padded[i, 2 * h + j, pl.ds(start, 64), :] for i, start in enumerate(starts)]
             blocks.append(functools.reduce(jnp.add, terms))
-        return jnp.concatenate(blocks, axis=1).reshape(4, 4, 16, 256)
+        return jnp.concatenate(blocks, axis=1).reshape(4, 16, 256)
 
     def placed_tiles(h, first):
         return placed(tile_pad, [384 - offset_ref[0, 0, t] + first for t in range(2)], h)
 
-    def reduced(source, s1, r1, core_number, acc, s2, r2, numbers):
-        copy = remote(core_number, s1, r1, across)
-        copy.start()
-        sent.append(copy)
+    def fill(source, s1, row):
         for h in range(2):
-            acc[:, :, h] = source(h, c * 256)
-        copy.wait_recv()
-        value = acc[...] + r1[...].astype(F32)
-        acc[...] = value
-        s2[...] = value.astype(BF)
+            s1[row, :, h] = source(h, (1 - c) * 256 + row * 64).astype(BF)
+
+    def reduced(source, filled, s1, r1, core_number, acc, s2, r2, numbers, beside):
+        swaps = []
+        for g, dx in enumerate(ROWS):
+            row = turn(x, dx)
+            if not filled:
+                fill(source, s1, row)
+            copy = remote(core_number + g, s1.at[row], r1.at[row], across)
+            copy.start()
+            swaps.append(copy)
+        beside()
+        for dx in ROWS:
+            row = turn(x, dx)
+            for h in range(2):
+                acc[row, :, h] = source(h, c * 256 + row * 64)
         copies = []
-        for i, (dx, dy) in enumerate(PLANE):
-            copy = remote(numbers + i, s2.at[turn(x, dx), turn(y, dy)], r2.at[i], plane[i])
-            copy.start()
-            copies.append(copy)
-        sent.extend(copies)
+        for g, dx in enumerate(ROWS):
+            row = turn(x, dx)
+            swaps[g].wait_recv()
+            value = acc[row] + r1[row].astype(F32)
+            acc[row] = value
+            s2[row] = value.astype(BF)
+            for i, (ex, dy) in enumerate(PLANE):
+                if ex == dx:
+                    copy = remote(numbers + i, s2.at[row, turn(y, dy)], r2.at[i], plane[i])
+                    copy.start()
+                    copies.append(copy)
+        sent.extend(swaps + copies)
         value = acc[x, y]
         for copy in copies:
             copy.wait_recv()
@@ -199,24 +214,31 @@
             value = value + r2[i].astype(F32)
         return value
 
-    def gathered(whole, numbers, core_number):
+    def gathered(whole, numbers, core_number, beside, use):
         copies = []
         block = whole.at[c, x, y]
         for i in range(len(PLANE)):
             copy = remote(numbers + i, block, block, plane[i])
             copy.start()
             copies.append(copy)
-        sent.extend(copies)
-        for copy in copies:
+        beside()
+        swaps = []
+        for g, dx in enumerate(ROWS[::-1]):
+            for i, (ex, dy) in enumerate(PLANE):
+                if ex == dx:
+                    copies[i].wait_recv()
+            block = whole.at[c, turn(x, 4 - dx)]
+            copy = remote(core_number + g, block, block, across)
+            copy.start()
+            swaps.append(copy)
+        sent.extend(copies + swaps)
+        use(0)
+        for copy in swaps:
             copy.wait_recv()
-        block = whole.at[c]
-        copy = remote(core_number, block, block, across)
-        copy.start()
-        sent.append(copy)
-        copy.wait_recv()
-
-    for h in range(2):
-        s1[:, :, h] = placed_tiles(h, (1 - c) * 256).astype(BF)
+        use(1)
+
+    for dx in ROWS:
+        fill(placed_tiles, s1, turn(x, dx))
 
     pl.semaphore_wait(barrier, 1 + len(PLANE) + len(COLUMN))
     sent = []
@@ -227,9 +249,9 @@
         for j, device in enumerate((right, left)):
             tile = t if j == 0 else 1 - t
             own = matrix_hbm.at[tile, quarter]
-            there = matrices.at[2 - 2 * j, tile, quarter]
+            there = matrices.at[3 - 2 * j, tile, quarter]
             if i // 4 == 1:
-                own, there = there, matrices.at[1, tile, quarter]
+                own, there = there, matrices.at[2, tile, quarter]
             steps.append(remote(MATS + 2 * i + j, own, there, device))
     arrived = set()
 
@@ -246,22 +268,26 @@
         copy = remote(OFFS + d - 1, offsets.at[0], offsets.at[4 - d], at(s=turn(s, d)))
         early.append(copy)
 
-    for copy in early:
-        copy.start()
-    go(BEFORE)
-    block = reduced(placed_tiles, s1, r1, CORE_P, acc1, s2, r2, RS_P)
+    def beside_first():
+        for copy in early:
+            copy.start()
+        go(BEFORE)
+
+    def widen(other):
+        half = c if other == 0 else 1 - c
+        for h in range(2):
+            projection = full[half, :, :, h].reshape(256, 256).astype(F32)
+            for j in range(2):
+                window[h, j, pl.ds(half * 256, 256), :] = projection[:, 128 * j : 128 * j + 128]
+
+    block = reduced(placed_tiles, True, s1, r1, CORE_P, acc1, s2, r2, RS_P, beside_first)
     sz[...] = block
     copy = remote(Z_P, sz, rz, at(zl=1 - zl))
     copy.start()
     sent.append(copy)
     copy.wait_recv()
-    go(BETWEEN)
     full[c, x, y] = (block + rz[...]).astype(BF)
-    gathered(full, AG_P, CORE_GP)
-    for h in range(2):
-        projection = full[:, :, :, h].reshape(512, 256).astype(F32)
-        for j in range(2):
-            window[h, j] = projection[:, 128 * j : 128 * j + 128]
+    gathered(full, AG_P, CORE_GP, lambda: go(BETWEEN), widen)
 
     for load in loads[2:]:
         load.wait()
@@ -298,9 +324,7 @@
     def placed_patches(h, first):
         return placed(grad_pad, [256 - position_ref[0, 0, 0, k] + first for k in range(CAP)], h)
 
-    for h in range(2):
-        t1[:, :, h] = placed_patches(h, (1 - c) * 256).astype(BF)
-    block = reduced(placed_patches, t1, q1, CORE_I, acc2, t2, q2, RS_I)
+    block = reduced(placed_patches, False, t1, q1, CORE_I, acc2, t2, q2, RS_I, lambda: None)
     for k in range(4):
         zs[k] = block[k // 2, :, 128 * (k % 2) : 128 * (k % 2) + 128]
     zr[0, 0] = zs[s]
@@ -312,19 +336,32 @@
     sent.extend(copies)
     for copy in copies:
         copy.wait_recv()
-    go([i for i in range(12) if i not in BEFORE and i not in BETWEEN])
     slabs[c, x, y] = (zr[0] + zr[1]).astype(BF)
-    gathered(slabs, AG_I, CORE_GI)
-
-    for copy in early:
-        copy.wait_recv()
-    columns = lax.broadcasted_iota(jnp.int32, (128, 512), 1) - lax.broadcasted_iota(jnp.int32, (128, 512), 0)
-    for k in range(4):
-        slab = slabs[:, :, :, k].reshape(512, 128)
-        for t in range(2):
-            first = jnp.broadcast_to(offsets[k, t][0:1, 0:1], (128, 512))
-            chosen = jnp.where(columns == first, 1.0, 0.0).astype(BF)
-            windows_out[t, 128 * k : 128 * k + 128, :] = dot(chosen, slab).astype(BF)
+
+    def beside_last():
+        go([i for i in range(12) if i not in BEFORE and i not in BETWEEN])
+        for copy in early:
+            copy.wait_recv()
+        distance = lax.broadcasted_iota(jnp.int32, (128, 256), 1) - lax.broadcasted_iota(jnp.int32, (128, 256), 0)
+        for other in range(2):
+            rows = distance + 256 * (c if other == 0 else 1 - c)
+            for k in range(4):
+                for t in range(2):
+                    first = jnp.broadcast_to(offsets[k, t][0:1, 0:1], (128, 256))
+                    picks[other, k, t] = jnp.where(rows == first, 1.0, 0.0).astype(BF)
+
+    def picked(other):
+        half = c if other == 0 else 1 - c
+        for k in range(4):
+            slab = slabs[half, :, :, k].reshape(256, 128)
+            for t in range(2):
+                value = dot(picks[other, k, t], slab)
+                if other == 0:
+                    own_rows[k, t] = value
+                else:
+                    windows_out[t, 128 * k : 128 * k + 128, :] = (own_rows[k, t] + value).astype(BF)
+
+    gathered(slabs, AG_I, CORE_GI, beside_last, picked)
     for i, copy in enumerate(steps):
         if i not in arrived:
             copy.wait_recv()
@@ -332,22 +369,13 @@
         copy.wait_send()
 
 
-def back_kernel(windows_hbm, own_hbm, matrices_hbm, out_hbm, windows, weights, out, load_sem, store_sem):
-    loads = [pltpu.make_async_copy(windows_hbm, windows, load_sem.at[4])]
-    for t in range(2):
-        loads += [
-            pltpu.make_async_copy(own_hbm.at[t], weights.at[t, 0], load_sem.at[2 * t]),
-            pltpu.make_async_copy(matrices_hbm.at[:, t], weights.at[t, pl.ds(1, 3)], load_sem.at[2 * t + 1]),
-        ]
-    for load in loads:
-        load.start()
-    for load in loads:
-        load.wait()
+def back_kernel(windows, matrices, out_hbm, out, store_sem):
     stores = []
     for quarter in range(4):
         lines = pl.ds(8 * quarter, 8)
         for t in range(2):
-            side = jnp.concatenate([weights[t, k, 256 * quarter : 256 * quarter + 256] for k in range(4)], axis=1)
+            rows = pl.ds(256 * quarter, 256)
+            side = jnp.concatenate([matrices[k, t, rows] for k in range(4)], axis=1)
             slope = (-STEP_LENGTH * dot(side, windows[t])).reshape(8, 32, 128)
             for part in range(2):
                 out[part, lines, 32 * t : 32 * t + 32, :] = slope[:, :, 64 * part : 64 * part + 64]
@@ -363,20 +391,21 @@
 
 def per_device(volume, tile_matrix, tile_offset, patch_count, scan_position, measured, illumination):
     any_space = pl.BlockSpec(memory_space=pl.ANY)
+    vmem = pl.BlockSpec(memory_space=pltpu.VMEM)
     smem = pl.BlockSpec(memory_space=pltpu.SMEM)
     block = (4, 4, 2, 16, 256)
     tile_matrix = tile_matrix.reshape(2, 1024, 128)
+    arrays = (volume, tile_matrix, measured.reshape(3, 256, 256), illumination, jnp.asarray(tables()))
     windows, matrices = pl.pallas_call(
         kernel,
         out_shape=(
-            jax.ShapeDtypeStruct((2, 512, 128), BF),
-            jax.ShapeDtypeStruct((3, 2, 1024, 128), BF),
+            pltpu.VMEM((2, 512, 128), BF),
+            pltpu.VMEM((4, 2, 1024, 128), BF),
         ),
         in_specs=[smem] * 3 + [any_space] * 5,
-        out_specs=(pl.BlockSpec(memory_space=pltpu.VMEM), any_space),
+        out_specs=(vmem, vmem),
         scratch_shapes=[
             pltpu.VMEM((2, 32, 64, 256), BF),
-            pltpu.VMEM((2, 1024, 128), BF),
             pltpu.VMEM((3, 256, 256), F32),
             pltpu.VMEM((2, 256, 256), F32),
             pltpu.VMEM((2, 512, 512), BF),
@@ -400,37 +429,32 @@
             pltpu.VMEM((4, 16, 128), F32),
             pltpu.VMEM((2, 4, 16, 128), F32),
             pltpu.VMEM((2, 4, 4, 4, 16, 128), BF),
+            pltpu.VMEM((2, 4, 2, 128, 256), BF),
+            pltpu.VMEM((4, 2, 128, 128), F32),
             pltpu.SemaphoreType.DMA((5,)),
             pltpu.SemaphoreType.DMA((N_SEMS,)),
             pltpu.SemaphoreType.DMA((N_SEMS,)),
         ],
         compiler_params=pltpu.CompilerParams(
-            collective_id=0, has_side_effects=True, vmem_limit_bytes=60 * 2**20
+            collective_id=0, has_side_effects=True, vmem_limit_bytes=44 * 2**20
         ),
     )(
-        tile_offset,
+        pltpu.with_memory_space_constraint(tile_offset, pltpu.HBM),
         patch_count,
-        jnp.swapaxes(scan_position, 2, 3),
-        volume,
-        tile_matrix,
-        measured.reshape(3, 256, 256),
-        illumination,
-        jnp.asarray(tables()),
+        pltpu.with_memory_space_constraint(jnp.swapaxes(scan_position, 2, 3), pltpu.HBM),
+        *(pltpu.with_memory_space_constraint(a, pltpu.HBM) for a in arrays),
     )
     return pl.pallas_call(
         back_kernel,
         out_shape=jax.ShapeDtypeStruct((2, 32, 64, 64), F32),
-        in_specs=[any_space] * 3,
+        in_specs=[vmem, vmem],
         out_specs=any_space,
         scratch_shapes=[
-            pltpu.VMEM((2, 512, 128), BF),
-            pltpu.VMEM((2, 4, 1024, 128), BF),
             pltpu.VMEM((2, 32, 64, 64), F32),
-            pltpu.SemaphoreType.DMA((5,)),
             pltpu.SemaphoreType.DMA((8,)),
         ],
-        compiler_params=pltpu.CompilerParams(vmem_limit_bytes=60 * 2**20),
-    )(windows, tile_matrix, matrices)
+        compiler_params=pltpu.CompilerParams(vmem_limit_bytes=44 * 2**20),
+    )(*(pltpu.with_memory_space_constraint(a, pltpu.VMEM) for a in (windows, matrices)))
 
 
 def solution(mesh):

time: 61.7 us -> 59.2 us (0.959)
  the two profiles are of different devices: /device:TPU:1 before, /device:TPU:32 now
where the time goes in v3:
time: 59.2 us; the launch traced here: 59.1 us
  Pallas kernels  58.4 us (99%)
  between operations  0.66 us (1%)
    pallas_call x1, Pallas kernels, per_device(): pl.pallas_call(kernel, out_shape=(pltpu.VMEM((2, 512, 128), BF), pltpu.VM...  56.7 us
    pallas_call x1, Pallas kernels, per_device(): pl.pallas_call(back_kernel, out_shape=jax.ShapeDtypeStruct((2, 32, 64, 64...  1.73 us

profile of v3, /device:TPU:32, one launch (start us, length us, event | category | flops | bytes accessed | tf_op | source)
XLA Modules:
  0.0 59.1 jit_solution(17905521608848842931)
XLA Ops:
  0.7 56.7 %shard_map.82 = (bf16[2,512,128]{2,1,0:T(8,128)(2,1)S(1)}, bf16[4,2,1024,128]{3,2,1,0:T(8,128)(2,1)S(1)}) custom-call(s32[1,1,2]{2,1,0:T(1,128)} %offset_ref.1, s32[1,1]{1,0:T(1,128)S(6)} %copy.9.count_ref, s32[1,1,2,3]{3,2,1,0:T(2,128)} %bitcast.5, bf16[2,32,64,256]{3,2,1,0:T(8,128)(2,1)} %volume_hbm.1, bf16[2,1024,128]{2,1,0:T(8,128)(2,1)} %bitcast.4, ...), custom_call_target="tpu_custom_call" | custom-call | tf_op jit(solution)/shard_map/pallas_call | solution.py:399
  57.3 1.7 %shard_map.83 = f32[2,32,64,64]{3,2,1,0:T(8,128)} custom-call(bf16[2,512,128]{2,1,0:T(8,128)(2,1)S(1)} %get-tuple-element.7.windows, bf16[4,2,1024,128]{3,2,1,0:T(8,128)(2,1)S(1)} %get-tuple-element.8.matrices), custom_call_target="tpu_custom_call" | custom-call | tf_op jit(solution)/shard_map/pallas_call | solution.py:447

commit v4 on v3

--- a/solution.py
+++ b/solution.py
@@ -334,12 +334,12 @@
         copy.start()
         copies.append(copy)
     sent.extend(copies)
+    go([i for i in range(12) if i not in BEFORE and i not in BETWEEN])
     for copy in copies:
         copy.wait_recv()
     slabs[c, x, y] = (zr[0] + zr[1]).astype(BF)
 
     def beside_last():
-        go([i for i in range(12) if i not in BEFORE and i not in BETWEEN])
         for copy in early:
             copy.wait_recv()
         distance = lax.broadcasted_iota(jnp.int32, (128, 256), 1) - lax.broadcasted_iota(jnp.int32, (128, 256), 0)

time: 59.2 us -> 58.9 us (level)
  the two profiles are of different devices: /device:TPU:32 before, /device:TPU:1 now
where the time goes in v4:
time: 58.9 us; the launch traced here: 58.8 us
  Pallas kernels  58.1 us (99%)
  between operations  0.66 us (1%)
    pallas_call x1, Pallas kernels, per_device(): pl.pallas_call(kernel, out_shape=(pltpu.VMEM((2, 512, 128), BF), pltpu.VM...  56.4 us
    pallas_call x1, Pallas kernels, per_device(): pl.pallas_call(back_kernel, out_shape=jax.ShapeDtypeStruct((2, 32, 64, 64...  1.73 us

profile of v4, /device:TPU:1, one launch (start us, length us, event | category | flops | bytes accessed | tf_op | source)
XLA Modules:
  0.0 58.8 jit_solution(3648188174378618269)
XLA Ops:
  0.7 56.4 %shard_map.82 = (bf16[2,512,128]{2,1,0:T(8,128)(2,1)S(1)}, bf16[4,2,1024,128]{3,2,1,0:T(8,128)(2,1)S(1)}) custom-call(s32[1,1,2]{2,1,0:T(1,128)} %offset_ref.1, s32[1,1]{1,0:T(1,128)S(6)} %copy.9.count_ref, s32[1,1,2,3]{3,2,1,0:T(2,128)} %bitcast.5, bf16[2,32,64,256]{3,2,1,0:T(8,128)(2,1)} %volume_hbm.1, bf16[2,1024,128]{2,1,0:T(8,128)(2,1)} %bitcast.4, ...), custom_call_target="tpu_custom_call" | custom-call | tf_op jit(solution)/shard_map/pallas_call | solution.py:399
  57.1 1.7 %shard_map.83 = f32[2,32,64,64]{3,2,1,0:T(8,128)} custom-call(bf16[2,512,128]{2,1,0:T(8,128)(2,1)S(1)} %get-tuple-element.7.windows, bf16[4,2,1024,128]{3,2,1,0:T(8,128)(2,1)S(1)} %get-tuple-element.8.matrices), custom_call_target="tpu_custom_call" | custom-call | tf_op jit(solution)/shard_map/pallas_call | solution.py:447
